TPU v7x, 1024 devices: a whole 4x4x32 slice. The times are simulated.
1024 devices in a mesh: cluster: 32 (over x, y, core), sample: 32 (over z).
Axes of the slice: x: 4, y: 4, z: 32, core: 2. Of those that a mesh axis runs over, the one named last changes fastest.
Arguments:
- child_pattern: float32 [2, 4096, 16384], P(None, 'cluster', 'sample'), may hold values from -6 to 6
- child_local: float32 [2, 4096, 16384], P(None, 'cluster', 'sample'), may hold values from -6 to 6
- interp_weight: float32 [6, 32768], P(None, 'sample'), may hold values from -0.1 to 0.3
- child_phase: float32 [8, 32768], P(None, 'sample'), may hold values from -3.140625 to 3.140625
- translator: float32 [316, 2, 32768], P(None, None, 'sample'), may hold values from -0.6 to 0.6
- partners: int32 [512, 64], replicated, may hold values from 0 to 511
- operator_id: int32 [512, 64], replicated, may hold values from 0 to 315
- list_len: int32 [512], replicated, may hold values from 8 to 64, as said below
Outputs:
- parent_incoming: float32 [2, 512, 32768], P(None, 'cluster', 'sample')
- child_incoming: float32 [2, 4096, 16384], P(None, 'cluster', 'sample')
Inputs may be any that keep to these rules, and one draw needn't show every extreme that they name: Parent q's interaction list is its first list_len[q] entries of partners and operator_id; later entries are unused.
All inputs are finite; a program needn't handle non-finite values.
Results may differ from a plain program's by a relative error of at most 0.0003.
Values sent between devices are 32-bit elements; how exact they have to be, the bound alone decides.
A program may use at most 32 MiB of HBM per device.

v0:
```python
import jax
import jax.numpy as jnp
from jax import lax
from jax.sharding import PartitionSpec as P

TAPS = 6
CHILDREN = 8


def with_halo(block, sides, width):
    for axis, dim in sides:
        count = lax.axis_size(axis)
        forward = [(i, i + 1) for i in range(count - 1)]
        forward.append((count - 1, 0))
        backward = [(target, source) for source, target in forward]
        low = lax.ppermute(
            lax.slice_in_dim(block, block.shape[dim] - width, None, axis=dim), axis, forward
        )
        high = lax.ppermute(lax.slice_in_dim(block, 0, width, axis=dim), axis, backward)
        block = jnp.concatenate([low, block, high], axis=dim)
    return block


def translate(pattern, table, partner_rows, operator_rows, lengths):
    receivers = partner_rows.shape[0]
    slot_count = partner_rows.shape[1]
    group_size = 16
    sample_count = pattern.shape[2]

    def advance(block, total):
        partner_cols = lax.dynamic_slice_in_dim(partner_rows, block * group_size, group_size, 1)
        operator_cols = lax.dynamic_slice_in_dim(operator_rows, block * group_size, group_size, 1)
        slot_index = block * group_size + jnp.arange(group_size)
        alive_mask = (slot_index[None, :] < lengths[:, None]).astype(jnp.float32)
        source = jnp.take(pattern, partner_cols, axis=1)
        coupling = jnp.take(table, operator_cols, axis=0)
        coup_real = coupling[:, :, 0] * alive_mask[:, :, None]
        coup_imag = coupling[:, :, 1] * alive_mask[:, :, None]
        real_part = jnp.sum(coup_real * source[0] - coup_imag * source[1], axis=1)
        imag_part = jnp.sum(coup_real * source[1] + coup_imag * source[0], axis=1)
        return total + jnp.stack([real_part, imag_part])

    start_total = jnp.zeros((2, receivers, sample_count), jnp.float32)
    return lax.fori_loop(0, slot_count // group_size, advance, start_total)


def phase_sum(upsampled, cosine, sine, parent_count):
    grouped = upsampled.reshape(2, parent_count, CHILDREN, upsampled.shape[2])
    real_part = jnp.sum(cosine[None] * grouped[0] - sine[None] * grouped[1], axis=1)
    imag_part = jnp.sum(cosine[None] * grouped[1] + sine[None] * grouped[0], axis=1)
    return jnp.stack([real_part, imag_part])


def phase_spread(incoming, cosine, sine):
    shifted_real = cosine[None] * incoming[0][:, None] + sine[None] * incoming[1][:, None]
    shifted_imag = cosine[None] * incoming[1][:, None] - sine[None] * incoming[0][:, None]
    return jnp.stack([shifted_real, shifted_imag]).reshape(2, -1, incoming.shape[2])


def local(
    child_pattern,
    child_local,
    interp_weight,
    child_phase,
    translator,
    partners,
    operator_id,
    list_len,
):
    rim_width = TAPS // 2
    child_count = child_pattern.shape[1]
    parent_count = child_count // CHILDREN
    half_samples = child_pattern.shape[2]
    cosine = jnp.cos(child_phase)
    sine = jnp.sin(child_phase)
    cos_even = cosine[:, 0::2]
    cos_odd = cosine[:, 1::2]
    sin_even = sine[:, 0::2]
    sin_odd = sine[:, 1::2]
    weight_even = interp_weight[:, 0::2]
    weight_odd = interp_weight[:, 1::2]
    padded = with_halo(child_pattern, (("sample", 2),), rim_width)
    up_even = jnp.zeros((2, child_count, half_samples), jnp.float32)
    up_odd = jnp.zeros((2, child_count, half_samples), jnp.float32)
    for tap in range(TAPS):
        window = padded[:, :, 1 + tap : 1 + tap + half_samples]
        up_even = up_even + weight_even[tap][None, None, :] * window
        up_odd = up_odd + weight_odd[tap][None, None, :] * window
    parent_even = phase_sum(up_even, cos_even, sin_even, parent_count)
    parent_odd = phase_sum(up_odd, cos_odd, sin_odd, parent_count)
    parent = jnp.stack([parent_even, parent_odd], axis=3).reshape(2, parent_count, 2 * half_samples)
    cluster_index = lax.axis_index("cluster")
    whole = lax.all_gather(parent, "cluster", axis=1, tiled=True)
    first_row = cluster_index * parent_count
    own_partners = lax.dynamic_slice_in_dim(partners, first_row, parent_count, 0)
    own_operators = lax.dynamic_slice_in_dim(operator_id, first_row, parent_count, 0)
    own_lengths = lax.dynamic_slice_in_dim(list_len, first_row, parent_count, 0)
    incoming = translate(whole, translator, own_partners, own_operators, own_lengths)
    shift_even = phase_spread(incoming[:, :, 0::2], cos_even, sin_even)
    shift_odd = phase_spread(incoming[:, :, 1::2], cos_odd, sin_odd)
    weighted = jnp.stack(
        [
            weight_even[tap][None, None, :] * shift_even
            + weight_odd[tap][None, None, :] * shift_odd
            for tap in range(TAPS)
        ]
    )
    padded_weighted = with_halo(weighted, (("sample", 3),), rim_width)
    child_incoming = child_local
    for tap in range(TAPS):
        offset = 2 * rim_width - 1 - tap
        child_incoming = child_incoming + padded_weighted[tap, :, :, offset : offset + half_samples]
    return (incoming, child_incoming)


def solution(mesh):
    placed = (
        P(None, "cluster", "sample"),
        P(None, "cluster", "sample"),
        P(None, "sample"),
        P(None, "sample"),
        P(None, None, "sample"),
        P(),
        P(),
        P(),
    )
    return jax.shard_map(
        local,
        mesh=mesh,
        in_specs=placed,
        out_specs=(P(None, "cluster", "sample"), P(None, "cluster", "sample")),
        check_vma=False,
    )
```

profile of v0, /device:TPU:1, one launch (start us, length us, event | category | flops | bytes accessed | tf_op | source)
XLA Modules:
  0.0 223.6 jit_solution(13014869103658431932)
XLA Ops:
  8.3 19.2 %collective-permute-start.1 = (f32[2,128,3]{2,1,0:T(8,128)S(1)}, f32[2,128,3]{2,1,0:T(8,128)S(1)}, u32[]{:S(2)}, u32[]{:S(2)}) collective-permute-start(f32[2,128,3]{2,1,0:T(8,128)S(1)} %get-tuple-element.187), channel_id=1, source_target_pairs={{1,0},{2,1},{3,2},{4,3},{5,4},{6,5},{7,6},{8,7},{9,8},{10,9},{11,1... | collective-permute-start | bytes 9224 | tf_op jit(solution)/shard_map/ppermute | solution.py:19
  27.6 1.9 collective-permute-start
  29.5 1.2 slice.209
  30.7 1.2 slice.191
  36.6 2.3 %multiply_add_fusion = f32[2,128,512]{2,1,0:T(8,128)S(1)} fusion(f32[2,128,512]{2,1,0:T(8,128)} %param.10, f32[2,128,515]{2,1,0:T(8,128)S(1)} %constant_dynamic-update-slice_fusion, f32[2,128,3]{2,1,0:T(8,128)S(1)} %collective-permute-done, f32[512]{0:T(512)S(1)} %bitcast.171, f32[512]{0:T(512)S(1)} %bitcast.173, f32[512]{0:T(512)S(1)} %bitcast.175, ...), kind=kLoop, calls=%fused_computation.54 | loop fusion | flops 1703936 | bytes 2636800 | tf_op jit(solution)/shard_map/add | solution.py:88
  43.7 74.1 %all-gather.2.cloned.1.call-done = f32[2,512,1024]{2,0,1:T(2,128)} async-done(((f32[2,16,1024]{2,0,1:T(2,128)}), f32[2,512,1024]{2,0,1:T(2,128)}) %all-gather.2.cloned.1.call-update) | async-done | bytes 4194320 | tf_op jit(solution)/shard_map/all_gather | solution.py:93
  117.8 67.1 %while.14 = (s32[]{:T(128)}, f32[2,16,1024]{2,1,0:T(8,128)S(1)}, s32[16,64]{0,1:T(8,128)S(1)}, f32[316,2,1024]{2,1,0:T(2,128)}, s32[16]{0:T(128)S(1)}, /*index=5...) while((s32[]{:T(128)}, f32[2,16,1024]{2,1,0:T(8,128)S(1)}, ...), condition=%wide.region_7.8_spmd.clone, body=%wide.region_4.7_spmd.clone.sunk | while | flops 3742743 | bytes 29918600 | solution.py:44
  118.0 5.0 %gather_fusion = f32[256,2,1024]{2,1,0:T(2,128)S(1)} fusion(f32[2,512,1024]{2,0,1:T(2,128)} %get-tuple-element.301, s32[1024]{0:T(1024)S(1)} %pad_clamp_fusion.4), kind=kCustom, calls=%fused_computation.1.clone.clone.1 | custom fusion | bytes 4195328 | tf_op jit(solution)/shard_map/while/body/eval_jaxpr/jit(_take)/gather | solution.py:35
  124.2 3.2 %fusion.32 = (f32[1,16,16,1024]{3,0,2,1:T(1,128)S(1)}, f32[1,16,16,1024]{3,0,2,1:T(1,128)}) fusion(f32[2,16,16,1024]{3,0,2,1:T(2,128)S(1)} %select_bitcast_fusion.2), kind=kLoop, calls=%fused_computation.87.clone.1 | loop fusion | bytes 4194304 | tf_op jit(solution)/shard_map/while/body/eval_jaxpr/slice | solution.py:39
  127.6 4.6 %gather_fusion.1 = f32[256,2,1024]{2,1,0:T(2,128)S(1)} fusion(f32[316,2,1024]{2,1,0:T(2,128)} %get-tuple-element.298, s32[1024]{0:T(1024)S(1)} %pad_clamp_fusion.5), kind=kCustom, calls=%fused_computation.clone.clone.1 | custom fusion | bytes 4195328 | tf_op jit(solution)/shard_map/while/body/eval_jaxpr/jit(_take)/gather | solution.py:36
  134.7 5.0 %gather_fusion = f32[256,2,1024]{2,1,0:T(2,128)S(1)} fusion(f32[2,512,1024]{2,0,1:T(2,128)} %get-tuple-element.301, s32[1024]{0:T(1024)S(1)} %pad_clamp_fusion.4), kind=kCustom, calls=%fused_computation.1.clone.clone.1 | custom fusion | bytes 4195328 | tf_op jit(solution)/shard_map/while/body/eval_jaxpr/jit(_take)/gather | solution.py:35
  140.9 3.2 %fusion.32 = (f32[1,16,16,1024]{3,0,2,1:T(1,128)S(1)}, f32[1,16,16,1024]{3,0,2,1:T(1,128)}) fusion(f32[2,16,16,1024]{3,0,2,1:T(2,128)S(1)} %select_bitcast_fusion.2), kind=kLoop, calls=%fused_computation.87.clone.1 | loop fusion | bytes 4194304 | tf_op jit(solution)/shard_map/while/body/eval_jaxpr/slice | solution.py:39
  144.3 4.6 %gather_fusion.1 = f32[256,2,1024]{2,1,0:T(2,128)S(1)} fusion(f32[316,2,1024]{2,1,0:T(2,128)} %get-tuple-element.298, s32[1024]{0:T(1024)S(1)} %pad_clamp_fusion.5), kind=kCustom, calls=%fused_computation.clone.clone.1 | custom fusion | bytes 4195328 | tf_op jit(solution)/shard_map/while/body/eval_jaxpr/jit(_take)/gather | solution.py:36
  151.4 5.0 %gather_fusion = f32[256,2,1024]{2,1,0:T(2,128)S(1)} fusion(f32[2,512,1024]{2,0,1:T(2,128)} %get-tuple-element.301, s32[1024]{0:T(1024)S(1)} %pad_clamp_fusion.4), kind=kCustom, calls=%fused_computation.1.clone.clone.1 | custom fusion | bytes 4195328 | tf_op jit(solution)/shard_map/while/body/eval_jaxpr/jit(_take)/gather | solution.py:35
  157.6 3.2 %fusion.32 = (f32[1,16,16,1024]{3,0,2,1:T(1,128)S(1)}, f32[1,16,16,1024]{3,0,2,1:T(1,128)}) fusion(f32[2,16,16,1024]{3,0,2,1:T(2,128)S(1)} %select_bitcast_fusion.2), kind=kLoop, calls=%fused_computation.87.clone.1 | loop fusion | bytes 4194304 | tf_op jit(solution)/shard_map/while/body/eval_jaxpr/slice | solution.py:39
  161.0 4.6 %gather_fusion.1 = f32[256,2,1024]{2,1,0:T(2,128)S(1)} fusion(f32[316,2,1024]{2,1,0:T(2,128)} %get-tuple-element.298, s32[1024]{0:T(1024)S(1)} %pad_clamp_fusion.5), kind=kCustom, calls=%fused_computation.clone.clone.1 | custom fusion | bytes 4195328 | tf_op jit(solution)/shard_map/while/body/eval_jaxpr/jit(_take)/gather | solution.py:36
  168.2 5.0 %gather_fusion = f32[256,2,1024]{2,1,0:T(2,128)S(1)} fusion(f32[2,512,1024]{2,0,1:T(2,128)} %get-tuple-element.301, s32[1024]{0:T(1024)S(1)} %pad_clamp_fusion.4), kind=kCustom, calls=%fused_computation.1.clone.clone.1 | custom fusion | bytes 4195328 | tf_op jit(solution)/shard_map/while/body/eval_jaxpr/jit(_take)/gather | solution.py:35
  174.3 3.2 %fusion.32 = (f32[1,16,16,1024]{3,0,2,1:T(1,128)S(1)}, f32[1,16,16,1024]{3,0,2,1:T(1,128)}) fusion(f32[2,16,16,1024]{3,0,2,1:T(2,128)S(1)} %select_bitcast_fusion.2), kind=kLoop, calls=%fused_computation.87.clone.1 | loop fusion | bytes 4194304 | tf_op jit(solution)/shard_map/while/body/eval_jaxpr/slice | solution.py:39
  177.7 4.6 %gather_fusion.1 = f32[256,2,1024]{2,1,0:T(2,128)S(1)} fusion(f32[316,2,1024]{2,1,0:T(2,128)} %get-tuple-element.298, s32[1024]{0:T(1024)S(1)} %pad_clamp_fusion.5), kind=kCustom, calls=%fused_computation.clone.clone.1 | custom fusion | bytes 4195328 | tf_op jit(solution)/shard_map/while/body/eval_jaxpr/jit(_take)/gather | solution.py:36
  184.9 2.2 slice.219
  187.1 2.2 slice.222
  189.4 1.6 fusion.22
  191.0 1.7 fusion.18
  195.5 1.5 fusion.25
  196.9 1.4 copy.50
  198.3 6.9 %collective-permute-start.2 = (f32[6,2,128,3]{2,1,3,0:T(2,128)S(1)}, f32[6,2,128,3]{2,1,3,0:T(2,128)S(1)}, u32[]{:S(2)}, u32[]{:S(2)}) collective-permute-start(f32[6,2,128,3]{2,1,3,0:T(2,128)S(1)} %copy.50), channel_id=1, source_target_pairs={{1,0},{2,1},{3,2},{4,3},{5,4},{6,5},{7,6},{8,7},{9,8},{10,9},{11,1... | collective-permute-start | bytes 55304 | tf_op jit(solution)/shard_map/ppermute | solution.py:19
  205.3 1.4 copy.52
  206.7 1.9 collective-permute-start.3
  208.6 1.2 copy.51
  209.8 2.5 %collective-permute-done.3 = f32[6,2,128,3]{2,1,3,0:T(2,128)S(1)} collective-permute-done((f32[6,2,128,3]{2,1,3,0:T(2,128)S(1)}, f32[6,2,128,3]{2,1,3,0:T(2,128)S(1)}, u32[]{:S(2)}, u32[]{:S(2)}) %collective-permute-start.3) | collective-permute-done | bytes 18464 | tf_op jit(solution)/shard_map/ppermute | solution.py:16
  212.4 1.2 copy.53
  213.6 3.2 %fusion.8 = f32[2,128,512]{2,1,0:T(8,128)} fusion(f32[6,2,128,512]{3,2,1,0:T(8,128)S(1)} %add_dynamic-update-slice_fusion, f32[6,2,128,3]{3,2,1,0:T(8,128)} %copy.53, f32[6,2,128,3]{3,2,1,0:T(8,128)} %copy.51, f32[2,128,512]{2,1,0:T(8,128)} %param.11, f32[1,128,512]{2,1,0:T(8,128)} %get-tuple-element.194, f32[1,128,512]{2,1,0:T(8,128)S(1)} %get-tuple-element.192, ...), kind=kLoop, calls=%fused_computation.31 | loop fusion | flops 2097152 | bytes 5283840 | tf_op jit(solution)/shard_map/add | solution.py:112
  (159 shorter events, 27.9 us)
Async XLA Ops:
  7.2 32.0 %copy-start.1 = (f32[2,128,512]{2,1,0:T(8,128)S(1)}, f32[2,128,512]{2,1,0:T(8,128)}, u32[]{:S(2)}) copy-start(f32[2,128,512]{2,1,0:T(8,128)} %param.10) | copy-start | bytes 1572868
  7.2 110.6 %all-gather.2.cloned.1.call-start = ((), (), s32[]{:S(2)}) async-start(), calls=%async_computation | async-start | bytes 4325376 | tf_op jit(solution)/shard_map/all_gather | solution.py:93
  8.3 28.2 %collective-permute-start.1 = (f32[2,128,3]{2,1,0:T(8,128)S(1)}, f32[2,128,3]{2,1,0:T(8,128)S(1)}, u32[]{:S(2)}, u32[]{:S(2)}) collective-permute-start(f32[2,128,3]{2,1,0:T(8,128)S(1)} %get-tuple-element.187), channel_id=1, source_target_pairs={{1,0},{2,1},{3,2},{4,3},{5,4},{6,5},{7,6},{8,7},{9,8},{10,9},{11,1... | collective-permute-start | bytes 9224 | tf_op jit(solution)/shard_map/ppermute | solution.py:19
  27.6 9.0 %collective-permute-start = (f32[2,128,3]{2,1,0:T(8,128)S(1)}, f32[2,128,3]{2,1,0:T(8,128)S(1)}, u32[]{:S(2)}, u32[]{:S(2)}) collective-permute-start(f32[2,128,3]{2,1,0:T(8,128)S(1)} %get-tuple-element.186), channel_id=1, source_target_pairs={{0,1},{1,2},{2,3},{3,4},{4,5},{5,6},{6,7},{7,8},{8,9},{9,10},{10,1... | collective-permute-start | bytes 9224 | tf_op jit(solution)/shard_map/ppermute | solution.py:16
  32.0 8.0 %copy-start.6 = (f32[1,512]{1,0:T(1,128)}, f32[1,512]{1,0:T(1,128)S(1)}, u32[]{:S(2)}) copy-start(f32[1,512]{1,0:T(1,128)S(1)} %get-tuple-element.212) | copy-start | bytes 6148
  32.0 8.0 %copy-start.10 = (f32[1,512]{1,0:T(1,128)}, f32[1,512]{1,0:T(1,128)S(1)}, u32[]{:S(2)}) copy-start(f32[1,512]{1,0:T(1,128)S(1)} %get-tuple-element.209) | copy-start | bytes 6148
  32.0 8.0 %copy-start.12 = (f32[1,512]{1,0:T(1,128)}, f32[1,512]{1,0:T(1,128)S(1)}, u32[]{:S(2)}) copy-start(f32[1,512]{1,0:T(1,128)S(1)} %get-tuple-element.210) | copy-start | bytes 6148
  32.0 8.0 %copy-start.14 = (f32[1,512]{1,0:T(1,128)}, f32[1,512]{1,0:T(1,128)S(1)}, u32[]{:S(2)}) copy-start(f32[1,512]{1,0:T(1,128)S(1)} %get-tuple-element.211) | copy-start | bytes 6148
  32.0 8.0 %copy-start.18 = (f32[1,512]{1,0:T(1,128)}, f32[1,512]{1,0:T(1,128)S(1)}, u32[]{:S(2)}) copy-start(f32[1,512]{1,0:T(1,128)S(1)} %get-tuple-element.213) | copy-start | bytes 6148
  32.0 8.0 %copy-start.19 = (f32[1,512]{1,0:T(1,128)}, f32[1,512]{1,0:T(1,128)S(1)}, u32[]{:S(2)}) copy-start(f32[1,512]{1,0:T(1,128)S(1)} %get-tuple-element.208) | copy-start | bytes 6148
  33.0 7.1 %copy-start.8 = (f32[1,512]{1,0:T(1,128)}, f32[1,512]{1,0:T(1,128)S(1)}, u32[]{:S(2)}) copy-start(f32[1,512]{1,0:T(1,128)S(1)} %get-tuple-element.206) | copy-start | bytes 6148
  33.0 7.1 %copy-start.16 = (f32[1,512]{1,0:T(1,128)}, f32[1,512]{1,0:T(1,128)S(1)}, u32[]{:S(2)}) copy-start(f32[1,512]{1,0:T(1,128)S(1)} %get-tuple-element.203) | copy-start | bytes 6148
  33.0 7.1 %copy-start.20 = (f32[1,512]{1,0:T(1,128)}, f32[1,512]{1,0:T(1,128)S(1)}, u32[]{:S(2)}) copy-start(f32[1,512]{1,0:T(1,128)S(1)} %get-tuple-element.204) | copy-start | bytes 6148
  33.0 7.1 %copy-start.22 = (f32[1,512]{1,0:T(1,128)}, f32[1,512]{1,0:T(1,128)S(1)}, u32[]{:S(2)}) copy-start(f32[1,512]{1,0:T(1,128)S(1)} %get-tuple-element.205) | copy-start | bytes 6148
  33.0 7.1 %copy-start.24 = (f32[1,512]{1,0:T(1,128)}, f32[1,512]{1,0:T(1,128)S(1)}, u32[]{:S(2)}) copy-start(f32[1,512]{1,0:T(1,128)S(1)} %get-tuple-element.207) | copy-start | bytes 6148
  33.0 7.1 %copy-start.25 = (f32[1,512]{1,0:T(1,128)}, f32[1,512]{1,0:T(1,128)S(1)}, u32[]{:S(2)}) copy-start(f32[1,512]{1,0:T(1,128)S(1)} %get-tuple-element.202) | copy-start | bytes 6148
  35.3 4.8 %copy-start.4 = (f32[8,512]{1,0:T(8,128)}, f32[8,512]{1,0:T(8,128)S(1)}, u32[]{:S(2)}) copy-start(f32[8,512]{1,0:T(8,128)S(1)} %slice.190) | copy-start | bytes 49156
  35.9 4.2 %copy-start.3 = (f32[8,512]{1,0:T(8,128)}, f32[8,512]{1,0:T(8,128)S(1)}, u32[]{:S(2)}) copy-start(f32[8,512]{1,0:T(8,128)S(1)} %slice.217) | copy-start | bytes 49156
  36.6 3.6 %copy-start.5 = (f32[8,512]{1,0:T(8,128)}, f32[8,512]{1,0:T(8,128)S(1)}, u32[]{:S(2)}) copy-start(f32[8,512]{1,0:T(8,128)S(1)} %slice.206) | copy-start | bytes 49156
  148.9 1.2 copy-start
  182.3 1.2 copy-start
  184.9 10.1 %copy-start.2 = (f32[2,16,1024]{2,1,0:T(8,128)}, f32[2,16,1024]{2,1,0:T(8,128)S(1)}, u32[]{:S(2)}) copy-start(f32[2,16,1024]{2,1,0:T(8,128)S(1)} %get-tuple-element.158) | copy-start | bytes 393220
  191.0 4.1 %copy-start.15 = (f32[1,512]{1,0:T(1,128)S(1)}, f32[1,512]{1,0:T(1,128)}, u32[]{:S(2)}) copy-start(f32[1,512]{1,0:T(1,128)} %copy-done.14) | copy-start | bytes 6148
  191.0 4.1 %copy-start.23 = (f32[1,512]{1,0:T(1,128)S(1)}, f32[1,512]{1,0:T(1,128)}, u32[]{:S(2)}) copy-start(f32[1,512]{1,0:T(1,128)} %copy-done.22) | copy-start | bytes 6148
  192.7 2.5 %copy-start.13 = (f32[1,512]{1,0:T(1,128)S(1)}, f32[1,512]{1,0:T(1,128)}, u32[]{:S(2)}) copy-start(f32[1,512]{1,0:T(1,128)} %copy-done.12) | copy-start | bytes 6148
  192.7 2.5 %copy-start.21 = (f32[1,512]{1,0:T(1,128)S(1)}, f32[1,512]{1,0:T(1,128)}, u32[]{:S(2)}) copy-start(f32[1,512]{1,0:T(1,128)} %copy-done.20) | copy-start | bytes 6148
  193.4 1.9 copy-start.11
  193.5 1.9 copy-start.17
  195.5 18.1 %copy-start.7 = (f32[1,512]{1,0:T(1,128)S(1)}, f32[1,512]{1,0:T(1,128)}, u32[]{:S(2)}) copy-start(f32[1,512]{1,0:T(1,128)} %copy-done.6) | copy-start | bytes 6148
  195.5 18.1 %copy-start.9 = (f32[1,512]{1,0:T(1,128)S(1)}, f32[1,512]{1,0:T(1,128)}, u32[]{:S(2)}) copy-start(f32[1,512]{1,0:T(1,128)} %copy-done.8) | copy-start | bytes 6148
  198.3 10.3 %collective-permute-start.2 = (f32[6,2,128,3]{2,1,3,0:T(2,128)S(1)}, f32[6,2,128,3]{2,1,3,0:T(2,128)S(1)}, u32[]{:S(2)}, u32[]{:S(2)}) collective-permute-start(f32[6,2,128,3]{2,1,3,0:T(2,128)S(1)} %copy.50), channel_id=1, source_target_pairs={{1,0},{2,1},{3,2},{4,3},{5,4},{6,5},{7,6},{8,7},{9,8},{10,9},{11,1... | collective-permute-start | bytes 55304 | tf_op jit(solution)/shard_map/ppermute | solution.py:19
  206.7 5.7 %collective-permute-start.3 = (f32[6,2,128,3]{2,1,3,0:T(2,128)S(1)}, f32[6,2,128,3]{2,1,3,0:T(2,128)S(1)}, u32[]{:S(2)}, u32[]{:S(2)}) collective-permute-start(f32[6,2,128,3]{2,1,3,0:T(2,128)S(1)} %copy.52), channel_id=1, source_target_pairs={{0,1},{1,2},{2,3},{3,4},{4,5},{5,6},{6,7},{7,8},{8,9},{9,10},{10,1... | collective-permute-start | bytes 55304 | tf_op jit(solution)/shard_map/ppermute | solution.py:16
  (2 other events, 2.5 us)
Sparse Core Ops, SparseCore 0:
  42.2 75.5 all-gather.1
where the time goes:
time: 225 us; the launch traced here: 224 us
  waiting for transfers between devices  76.7 us (34%)
  local copies, waits for them, and re-layouts  76.4 us (34%)
  starting transfers between devices  30 us (13%)
  other arithmetic  25.3 us (11%)
  between operations  14.6 us (6%)
    all_gather x1, waiting for transfers between devices, local(): whole = lax.all_gather(parent, 'cluster', axis=1, tiled=True)  74.1 us
    ppermute x2, starting transfers between devices, with_halo(): lax.ppermute(lax.slice_in_dim(block, 0, width, axis=dim), axis, backward)  26.2 us
    gather x4, local copies, waits for them, and re-layouts, advance(): source = jnp.take(pattern, partner_cols, axis=1)  20.2 us
    gather x4, local copies, waits for them, and re-layouts, advance(): coupling = jnp.take(table, operator_cols, axis=0)  18.3 us
    slice x4, local copies, waits for them, and re-layouts, advance(): real_part = jnp.sum(coup_real * source[0] - coup_imag * source[1], axis=1)  13 us
  transfers between devices with their start and end apart: 5, of which 2 were waited for; matrix products, arithmetic and copies ran while one was open for 5% of the time, Pallas kernels for 0%

commit v1 on v0

v1 whole, which is shorter than its diff:
```python
import functools

import jax
import jax.numpy as jnp
from jax import lax
from jax.experimental import pallas as pl
from jax.experimental.pallas import tpu as pltpu
from jax.sharding import PartitionSpec as P

TAPS = 6
CHILDREN = 8
PAR = 16
NT = 316
LMAX = 64
MESH = pl.DeviceIdType.MESH
CHUNK_OF = {0: (0, 0), 3: (0, 2), 2: (1, 0), 1: (1, 2)}


def lanes():
    return lax.broadcasted_iota(jnp.int32, (8, 128), 1)


def subs():
    return lax.broadcasted_iota(jnp.int32, (8, 128), 0)


def take(v, index):
    return jnp.take_along_axis(v, index, axis=1)


def split_pairs(v0, v1):
    lane = lanes()
    even = (2 * lane) % 128
    return tuple(
        jnp.where(lane < 64, take(v0, even + odd), take(v1, even + odd)) for odd in (0, 1)
    )


def join_pairs(e, o):
    lane = lanes()
    made = []
    for half in (0, 64):
        at = half + lane // 2
        made.append(jnp.where(lane % 2 == 0, take(e, at), take(o, at)))
    return made


def pack_low(groups):
    lane = lanes()
    total = jnp.zeros((8, 128), jnp.float32)
    for g, v in enumerate(groups):
        total = jnp.where(lane // 4 == g, pltpu.roll(v, 4 * g, 1) if g else v, total)
    return total


def pack_high(groups):
    lane = lanes()
    total = jnp.zeros((8, 128), jnp.float32)
    for g, v in enumerate(groups):
        shift = (4 * g + 4) % 128
        total = jnp.where(lane // 4 == g, pltpu.roll(v, shift, 1) if shift else v, total)
    return total


def as_high_halo(packed, g):
    return pltpu.roll(packed, (128 - 4 * g) % 128, 1) if g else packed


def as_low_halo(packed, g):
    shift = (128 - (4 * g + 4)) % 128
    return pltpu.roll(packed, shift, 1) if shift else packed


def kernel(
    cp, cl, w, ph, t, part, oper, length,
    out0, out1,
    p_0, p_1, ab_0, ab_1, inc_0, inc_1, tv, xpad, clv, wv, phv, wpad, phpad, cs, wb, agg, incpad,
    opv, opm, pidx, oidx, lens,
    halo_out, halo_in, edge_out, edge_in,
    load_sem, index_sem, send_sem, row_sem, col_sem, twin_sem, halo_send, halo_recv, edge_send, edge_recv,
):
    gathered, tables, incoming = (p_0, p_1), (ab_0, ab_1), (inc_0, inc_1)
    me = lax.axis_index("cluster")
    z = lax.axis_index("sample")
    core = me % 2
    y = (me // 2) % 4
    x = me // 8
    step_a = 8 - 6 * core
    step_b = 2 + 6 * core
    at_a = x * (1 - core) + y * core
    at_b = y * (1 - core) + x * core
    twin = me + 1 - 2 * core

    def dev(da, db):
        return step_a * ((at_a + da + 4) % 4) + step_b * ((at_b + db + 4) % 4) + core

    z_low = (z + 31) % 32
    z_high = (z + 1) % 32

    first_row = pl.multiple_of(me * PAR, PAR)
    loads = [
        pltpu.make_async_copy(w, wv, load_sem.at[0]),
        pltpu.make_async_copy(ph, phv, load_sem.at[1]),
        pltpu.make_async_copy(cp, xpad.at[:, :, pl.ds(128, 512)], load_sem.at[2]),
        pltpu.make_async_copy(oper.at[pl.ds(first_row, PAR)], opv, load_sem.at[3]),
        pltpu.make_async_copy(length, lens, load_sem.at[4]),
        pltpu.make_async_copy(part.at[pl.ds(first_row, PAR)], pidx, load_sem.at[5]),
        pltpu.make_async_copy(t, tv, load_sem.at[6]),
        pltpu.make_async_copy(cl, clv, load_sem.at[7]),
    ]
    for load in loads:
        load.start()

    barrier = pltpu.get_barrier_semaphore()
    for there in (dev(1, 0), dev(-1, 0), dev(0, 1), dev(0, -1), twin):
        pl.semaphore_signal(barrier, inc=1, device_id={"cluster": there}, device_id_type=MESH)
    for there in (z_low, z_high):
        pl.semaphore_signal(barrier, inc=1, device_id={"sample": there}, device_id_type=MESH)

    loads[0].wait()
    loads[1].wait()
    for b in range(4):
        main = pl.ds(128 * (b + 1), 128)
        halves = []
        for k in (2 * b, 2 * b + 1):
            halves.append(
                jnp.concatenate([wv[:, 128 * k : 128 * (k + 1)], jnp.zeros((2, 128), jnp.float32)], 0)
            )
        for odd, v in enumerate(split_pairs(*halves)):
            wpad[odd, :, main] = v
        for odd, v in enumerate(
            split_pairs(
                phv[:, 256 * b : 256 * b + 128],
                phv[:, 256 * b + 128 : 256 * b + 256],
            )
        ):
            phpad[odd, :, main] = v

    loads[2].wait()

    def ends(block, packer):
        here = pl.ds(128 * (block + 1), 128)
        children = [xpad[c, 8 * p : 8 * p + 8, here] for c in range(2) for p in range(PAR)]
        others = [wpad[0, :, here], wpad[1, :, here], phpad[0, :, here], phpad[1, :, here]]
        return packer(children), packer(others)

    halo_out[0, 0], halo_out[0, 1] = ends(0, pack_low)
    halo_out[1, 0], halo_out[1, 1] = ends(3, pack_high)
    pl.semaphore_wait(barrier, 7)
    halos = [
        pltpu.make_async_remote_copy(
            src_ref=halo_out.at[side],
            dst_ref=halo_in.at[side],
            send_sem=halo_send.at[side],
            recv_sem=halo_recv.at[side],
            device_id={"sample": there},
            device_id_type=MESH,
        )
        for side, there in ((0, z_low), (1, z_high))
    ]
    for halo in halos:
        halo.start()

    for odd in range(2):
        cs[0, odd, :, 128:640] = jnp.cos(phpad[odd, :, 128:640])
        cs[1, odd, :, 128:640] = jnp.sin(phpad[odd, :, 128:640])

    def broadcast_weights(blocks):
        for odd in range(2):
            for tap in range(TAPS):
                for blk in blocks:
                    here = pl.ds(128 * blk, 128)
                    wb[odd, tap, :, here] = jnp.broadcast_to(wpad[odd, tap : tap + 1, here], (8, 128))

    broadcast_weights(range(1, 5))

    def aggregate(b):
        main = pl.ds(128 * (b + 1), 128)
        weight = [[wb[odd, tap, :, main] for tap in range(TAPS)] for odd in range(2)]
        cosine = [cs[0, odd, :, main] for odd in range(2)]
        sine = [cs[1, odd, :, main] for odd in range(2)]

        def one(p, _):
            rows = pl.ds(pl.multiple_of(8 * p, 8), 8)
            up = []
            for c in range(2):
                wide = xpad[c, rows, pl.ds(128 * b, 384)]
                window = [wide[:, 126 + tap : 254 + tap] for tap in range(TAPS)]
                up.append(
                    [sum(weight[odd][tap] * window[tap] for tap in range(TAPS)) for odd in range(2)]
                )
            for odd in range(2):
                real = cosine[odd] * up[0][odd] - sine[odd] * up[1][odd]
                imag = cosine[odd] * up[1][odd] + sine[odd] * up[0][odd]
                agg[b, odd, 0, pl.ds(p, 1), :] = jnp.sum(real, axis=0, keepdims=True)
                agg[b, odd, 1, pl.ds(p, 1), :] = jnp.sum(imag, axis=0, keepdims=True)
            return 0

        lax.fori_loop(0, PAR, one, 0)
        chunk, place = CHUNK_OF[b]
        for c in range(2):
            for i in range(2):
                pieces = [agg[b, odd, c, 8 * i : 8 * i + 8, :] for odd in range(2)]
                for half, v in enumerate(join_pairs(*pieces)):
                    gathered[chunk][pl.ds(me * PAR + 8 * i, 8), 2 * (place + half) + c, :] = v

    def block(h, d):
        return gathered[h].at[pl.ds(d * PAR, PAR)]

    def send(h, d, target, arrived):
        pltpu.make_async_remote_copy(
            src_ref=block(h, d),
            dst_ref=block(h, d),
            send_sem=send_sem.at[h],
            recv_sem=arrived,
            device_id={"cluster": target},
            device_id_type=MESH,
        ).start()

    def arrive(h, d, arrived):
        pltpu.make_async_remote_copy(
            src_ref=block(h, d),
            dst_ref=block(h, d),
            send_sem=send_sem.at[h],
            recv_sem=arrived,
            device_id={"cluster": twin},
            device_id_type=MESH,
        ).wait_recv()

    def give_twin(h, d):
        send(h, d, twin, twin_sem.at[h])

    OFF = (0, -1, 1, 2)

    def spread_b(h, g):
        d = dev(OFF[g], 0)
        send(h, d, dev(0, 1), col_sem.at[h, g, 0])
        send(h, d, dev(0, -1), col_sem.at[h, g, 1])

    def own(h):
        send(h, me, dev(1, 0), row_sem.at[h, 0])
        send(h, me, dev(-1, 0), row_sem.at[h, 1])
        spread_b(h, 0)
        give_twin(h, me)

    def row_events(h):
        for side, da in ((0, -1), (1, 1)):
            arrive(h, dev(da, 0), row_sem.at[h, side])
            if side == h:
                send(h, dev(da, 0), dev(-da, 0), row_sem.at[h, 2])
            spread_b(h, 1 + side)
            give_twin(h, dev(da, 0))

    def row_far(h):
        arrive(h, dev(2, 0), row_sem.at[h, 2])
        spread_b(h, 3)
        give_twin(h, dev(2, 0))

    def col_near(h, g):
        for side, db in ((0, -1), (1, 1)):
            d = dev(OFF[g], db)
            arrive(h, d, col_sem.at[h, g, side])
            if side == h:
                send(h, d, dev(0, -db), col_sem.at[h, g, 2])
            give_twin(h, d)

    def col_far(h, g):
        d = dev(OFF[g], 2)
        arrive(h, d, col_sem.at[h, g, 2])
        give_twin(h, d)

    def twin_all(h):
        half = gathered[h].at[pl.ds(0, 256)]
        pltpu.make_async_remote_copy(
            src_ref=half, dst_ref=half, send_sem=send_sem.at[h], recv_sem=twin_sem.at[h],
            device_id={"cluster": twin}, device_id_type=MESH,
        ).wait_recv()

    def sent_all(h):
        most = gathered[h].at[pl.ds(0, 31 * PAR)]
        pltpu.make_async_remote_copy(
            src_ref=most, dst_ref=most, send_sem=send_sem.at[h], recv_sem=twin_sem.at[h],
            device_id={"cluster": twin}, device_id_type=MESH,
        ).wait_send()

    def prepare_table(start, stop):
        def one(o, _):
            sub = subs()
            t0 = tv[o, 0:8, :]
            t1 = tv[o, 8:16, :]
            for ab, v in ((ab_0, jnp.where(sub < 4, t0, t1)), (ab_1, jnp.where(sub < 4, t1, t0))):
                ab[o, 0:8, :] = jnp.where(sub % 2 == 0, v, pltpu.roll(v, 1, 0))
                ab[o, 8:16, :] = jnp.where(sub % 2 == 0, pltpu.roll(v, 7, 0), -v)
            return 0

        lax.fori_loop(start, stop, one, 0)

    def translate(h, start, stop):
        def one(q, _):
            first = [jnp.zeros((8, 128), jnp.float32) for _ in range(2)]
            second = [jnp.zeros((8, 128), jnp.float32) for _ in range(2)]
            for slot in range(LMAX):
                source = gathered[h][pidx[q, slot]]
                o = oidx[q, slot]
                first[slot % 2] += tables[h][o, 0:8, :] * source
                second[slot % 2] += tables[h][o, 8:16, :] * source
            cross = second[0] + second[1]
            swapped = jnp.where(subs() % 2 == 0, pltpu.roll(cross, 7, 0), pltpu.roll(cross, 1, 0))
            incoming[h][pl.ds(pl.multiple_of(8 * q, 8), 8), :] = first[0] + first[1] + swapped
            return 0

        lax.fori_loop(start, stop, one, 0)

    def take_out(h):
        for b in range(4):
            chunk, place = CHUNK_OF[b]
            if chunk != h:
                continue
            for c in range(2):
                for i in range(2):
                    pieces = []
                    for half in range(2):
                        v = incoming[h][pl.ds(64 * i + 2 * (place + half) + c, 8, stride=8), :]
                        out0[c, 8 * i : 8 * i + 8, pl.ds(128 * (2 * b + half), 128)] = v
                        pieces.append(v)
                    for odd, v in enumerate(split_pairs(*pieces)):
                        incpad[b + 1, odd, c, 8 * i : 8 * i + 8, :] = v

    GROUPS = [(odd, c, i) for odd in range(2) for c in range(2) for i in range(2)]

    aggregate(2)
    aggregate(1)
    own(1)
    loads[3].wait()
    loads[4].wait()
    live = jnp.zeros((PAR, LMAX), jnp.int32)
    row = lax.broadcasted_iota(jnp.int32, (PAR, LMAX), 0)
    for i in range(PAR):
        live = jnp.where(row == i, lens[me * PAR + i], live)
    slot = lax.broadcasted_iota(jnp.int32, (PAR, LMAX), 1)
    opm[...] = jnp.where(slot < live, opv[...], NT)
    to_smem = pltpu.make_async_copy(opm, oidx, index_sem)
    to_smem.start()

    for halo in halos:
        halo.wait_recv()
    for c in range(2):
        for p in range(PAR):
            g = PAR * c + p
            xpad[c, 8 * p : 8 * p + 8, 640:768] = as_high_halo(halo_in[0, 0], g)
            xpad[c, 8 * p : 8 * p + 8, 0:128] = as_low_halo(halo_in[1, 0], g)
    aggregate(0)
    aggregate(3)
    own(0)

    for g, padded in enumerate((wpad, wpad, phpad, phpad)):
        padded[g % 2, :, 640:768] = as_high_halo(halo_in[0, 1], g)
        padded[g % 2, :, 0:128] = as_low_halo(halo_in[1, 1], g)
    for odd in range(2):
        for here in (slice(0, 128), slice(640, 768)):
            cs[0, odd, :, here] = jnp.cos(phpad[odd, :, here])
            cs[1, odd, :, here] = jnp.sin(phpad[odd, :, here])
    broadcast_weights((0, 5))

    for ab in tables:
        ab[NT] = jnp.zeros((16, 128), jnp.float32)
    loads[6].wait()
    row_events(0)
    prepare_table(0, 40)
    row_events(1)
    prepare_table(40, 80)
    col_near(0, 0)
    prepare_table(80, 120)
    row_far(0)
    row_far(1)
    prepare_table(120, 160)
    col_near(0, 1)
    prepare_table(160, 200)
    col_near(0, 2)
    col_far(0, 0)
    prepare_table(200, 240)
    col_near(1, 0)
    col_near(0, 3)
    prepare_table(240, 280)
    col_far(0, 1)
    col_near(1, 1)
    prepare_table(280, 316)
    col_far(0, 2)
    col_near(1, 2)
    col_far(0, 3)
    to_smem.wait()
    loads[5].wait()
    twin_all(0)
    translate(0, 0, 4)
    col_near(1, 3)
    col_far(1, 0)
    translate(0, 4, 8)
    col_far(1, 1)
    translate(0, 8, 12)
    col_far(1, 2)
    translate(0, 12, 16)
    col_far(1, 3)
    take_out(0)
    edge_out[0] = pack_low([incpad[1, odd, c, 8 * i : 8 * i + 8, :] for odd, c, i in GROUPS])
    edge_out[1] = pack_high([incpad[4, odd, c, 8 * i : 8 * i + 8, :] for odd, c, i in GROUPS])
    edges = [
        pltpu.make_async_remote_copy(
            src_ref=edge_out.at[side],
            dst_ref=edge_in.at[side],
            send_sem=edge_send.at[side],
            recv_sem=edge_recv.at[side],
            device_id={"sample": there},
            device_id_type=MESH,
        )
        for side, there in ((0, z_low), (1, z_high))
    ]
    for edge in edges:
        edge.start()
    twin_all(1)
    translate(1, 0, 16)
    take_out(1)
    for edge in edges:
        edge.wait_recv()
    for g, (odd, c, i) in enumerate(GROUPS):
        incpad[5, odd, c, 8 * i : 8 * i + 8, :] = as_high_halo(edge_in[0], g)
        incpad[0, odd, c, 8 * i : 8 * i + 8, :] = as_low_halo(edge_in[1], g)
    loads[7].wait()

    def disaggregate(p, _):
        rows = pl.ds(pl.multiple_of(8 * p, 8), 8)
        moved = []
        for odd in range(2):
            real, imag = (
                jnp.concatenate(
                    [jnp.broadcast_to(incpad[blk, odd, c, pl.ds(p, 1), :], (8, 128)) for blk in range(6)], 1
                )
                for c in range(2)
            )
            cosine, sine = cs[0, odd], cs[1, odd]
            moved.append((cosine * real + sine * imag, cosine * imag - sine * real))
        for c in range(2):
            total = clv[c, rows, :]
            for tap in range(TAPS):
                v = wb[0, tap] * moved[0][c] + wb[1, tap] * moved[1][c]
                shift = (tap - 2) % 768
                v = pltpu.roll(v, shift, 1) if shift else v
                total = total + v[:, 128:640]
            out1[c, rows, :] = total
        return 0

    lax.fori_loop(0, PAR, disaggregate, 0)

    for halo in halos:
        halo.wait_send()
    for edge in edges:
        edge.wait_send()
    sent_all(0)
    sent_all(1)


def local(child_pattern, child_local, interp_weight, child_phase, translator, partners, operator_id, list_len):
    operators = translator.shape[0]
    folded = translator.reshape(operators, 2, 8, 128).transpose(0, 2, 1, 3).reshape(operators, 16, 128)
    f32 = jnp.float32
    any_spec = pl.BlockSpec(memory_space=pl.ANY)
    vmem_spec = pl.BlockSpec(memory_space=pltpu.VMEM)
    return pl.pallas_call(
        kernel,
        out_shape=(
            jax.ShapeDtypeStruct((2, PAR, 1024), f32),
            jax.ShapeDtypeStruct((2, 128, 512), f32),
        ),
        in_specs=[any_spec] * 8,
        out_specs=(vmem_spec, vmem_spec),
        scratch_shapes=[
            pltpu.VMEM((512, 8, 128), f32),
            pltpu.VMEM((512, 8, 128), f32),
            pltpu.VMEM((320, 16, 128), f32),
            pltpu.VMEM((320, 16, 128), f32),
            pltpu.VMEM((128, 128), f32),
            pltpu.VMEM((128, 128), f32),
            pltpu.VMEM((316, 16, 128), f32),
            pltpu.VMEM((2, 128, 768), f32),
            pltpu.VMEM((2, 128, 512), f32),
            pltpu.VMEM((6, 1024), f32),
            pltpu.VMEM((8, 1024), f32),
            pltpu.VMEM((2, 8, 768), f32),
            pltpu.VMEM((2, 8, 768), f32),
            pltpu.VMEM((2, 2, 8, 768), f32),
            pltpu.VMEM((2, 6, 8, 768), f32),
            pltpu.VMEM((4, 2, 2, 16, 128), f32),
            pltpu.VMEM((6, 2, 2, 16, 128), f32),
            pltpu.VMEM((16, 64), jnp.int32),
            pltpu.VMEM((16, 64), jnp.int32),
            pltpu.SMEM((16, 64), jnp.int32),
            pltpu.SMEM((16, 64), jnp.int32),
            pltpu.SMEM((512,), jnp.int32),
            pltpu.VMEM((2, 2, 8, 128), f32),
            pltpu.VMEM((2, 2, 8, 128), f32),
            pltpu.VMEM((2, 8, 128), f32),
            pltpu.VMEM((2, 8, 128), f32),
            pltpu.SemaphoreType.DMA((8,)),
            pltpu.SemaphoreType.DMA,
            pltpu.SemaphoreType.DMA((2,)),
            pltpu.SemaphoreType.DMA((2, 3)),
            pltpu.SemaphoreType.DMA((2, 4, 3)),
            pltpu.SemaphoreType.DMA((2,)),
            pltpu.SemaphoreType.DMA((2,)),
            pltpu.SemaphoreType.DMA((2,)),
            pltpu.SemaphoreType.DMA((2,)),
            pltpu.SemaphoreType.DMA((2,)),
        ],
        compiler_params=pltpu.CompilerParams(
            collective_id=0, has_side_effects=True, vmem_limit_bytes=48 * 1024 * 1024
        ),
    )(child_pattern, child_local, interp_weight, child_phase, folded, partners, operator_id, list_len)


def solution(mesh):
    placed = (
        P(None, "cluster", "sample"),
        P(None, "cluster", "sample"),
        P(None, "sample"),
        P(None, "sample"),
        P(None, None, "sample"),
        P(),
        P(),
        P(),
    )
    return jax.shard_map(
        local,
        mesh=mesh,
        in_specs=placed,
        out_specs=(P(None, "cluster", "sample"), P(None, "cluster", "sample")),
        check_vma=False,
    )
```

time: 225 us -> 65.1 us (0.29)
  waiting for transfers between devices: 76.7 us -> 0 us
  local copies, waits for them, and re-layouts: 76.4 us -> 9.51 us
  Pallas kernels: 0 us -> 54.5 us
  starting transfers between devices: 30 us -> 0 us
  other arithmetic: 25.3 us -> 0 us
  between operations: 14.6 us -> 0.67 us
    all_gather x1 -> x0, waiting for transfers between devices: 74.1 us -> none  [local(): whole = lax.all_gather(parent, 'cluster', axis=1, tiled=True)]
    pallas_call x0 -> x1, Pallas kernels: none -> 54.5 us  [local(): pl.pallas_call(kernel, out_shape=(jax.ShapeDtypeStruct((2, PAR, 1024), f3...]
    gather x8 -> x0, local copies, waits for them, and re-layouts: 38.5 us -> none  [the longest x4 20.2 us: advance(): source = jnp.take(pattern, partner_cols, axis=1)]
    ppermute x4 -> x0, starting transfers between devices: 30 us -> none  [the longest x2 26.2 us: with_halo(): lax.ppermute(lax.slice_in_dim(block, 0, width, axis=dim), axis, backward)]
    slice x18 -> x0, local copies, waits for them, and re-layouts: 27.7 us -> none  [the longest x4 13 us: advance(): real_part = jnp.sum(coup_real * source[0] - coup_imag * source[1], axis=1)]
    add x13 -> x0, other arithmetic: 9.79 us -> none  [the longest x2 3.28 us: phase_spread(): cosine[None] * incoming[0][:, None] + sine[None] * incoming[1][:, None]]
    unnamed x51 -> x16, local copies, waits for them, and re-layouts: 1.19 us -> 9.51 us
    select_n x16 -> x0, other arithmetic: 7.77 us -> none  [the longest x8 4.44 us: advance(): source = jnp.take(pattern, partner_cols, axis=1)]
  transfers between devices with their start and end apart: 5 -> 0, of which waited for: 2 -> 0; matrix products, arithmetic and copies ran while one was open for 5% -> 0% of each run, Pallas kernels for 0% -> 0%
where the time goes in v1:
time: 65.1 us; the launch traced here: 64.7 us
  Pallas kernels  54.5 us (84%)
  local copies, waits for them, and re-layouts  9.51 us (15%)
  between operations  0.67 us (1%)
    pallas_call x1, Pallas kernels, local(): pl.pallas_call(kernel, out_shape=(jax.ShapeDtypeStruct((2, PAR, 1024), f3...  54.5 us
    unnamed x16, local copies, waits for them, and re-layouts  9.51 us

profile of v1, /device:TPU:1, one launch (start us, length us, event | category | flops | bytes accessed | tf_op | source)
XLA Modules:
  0.0 64.7 jit_solution(7089841323402264426)
XLA Ops:
  0.6 1.0 %copy.11.part = s32[512,64]{1,0:T(8,128)S(1)} copy(s32[512,64]{0,1:T(8,128)} %param.13) | data formatting | bytes 262144 | tf_op args[5]
  1.7 1.0 %copy.12.oper = s32[512,64]{1,0:T(8,128)S(1)} copy(s32[512,64]{0,1:T(8,128)} %param.14) | data formatting | bytes 262144 | tf_op args[6]
  2.7 0.0 copy-start
  2.7 1.7 %copy-done = f32[316,2,1024]{2,1,0:T(2,128)S(1)} copy-done((f32[316,2,1024]{2,1,0:T(2,128)S(1)}, f32[316,2,1024]{2,1,0:T(2,128)}, u32[]{:S(2)}) %copy-start) | copy-done | bytes 2588696
  4.4 0.0 copy-start.1
  4.4 1.0 %copy-done.1 = f32[2,128,512]{2,1,0:T(8,128)S(1)} copy-done((f32[2,128,512]{2,1,0:T(8,128)S(1)}, f32[2,128,512]{2,1,0:T(8,128)}, u32[]{:S(2)}) %copy-start.1) | copy-done | bytes 524312
  5.5 0.0 copy-start.2
  5.5 1.0 %copy-done.2 = f32[2,128,512]{2,1,0:T(8,128)S(1)} copy-done((f32[2,128,512]{2,1,0:T(8,128)S(1)}, f32[2,128,512]{2,1,0:T(8,128)}, u32[]{:S(2)}) %copy-start.2) | copy-done | bytes 524312
  6.5 0.0 copy-start.3
  6.5 0.8 %copy-done.3 = f32[6,1024]{1,0:T(8,128)S(1)} copy-done((f32[6,1024]{1,0:T(8,128)S(1)}, f32[6,1024]{1,0:T(8,128)}, u32[]{:S(2)}) %copy-start.3) | copy-done | bytes 24600
  7.3 0.0 copy-start.4
  7.3 0.8 %copy-done.4 = f32[8,1024]{1,0:T(8,128)S(1)} copy-done((f32[8,1024]{1,0:T(8,128)S(1)}, f32[8,1024]{1,0:T(8,128)}, u32[]{:S(2)}) %copy-start.4) | copy-done | bytes 32792
  8.0 0.0 copy-start.5
  8.0 0.7 %copy-done.5 = s32[512]{0:T(512)S(1)} copy-done((s32[512]{0:T(512)S(1)}, s32[512]{0:T(512)}, u32[]{:S(2)}) %copy-start.5) | copy-done | bytes 2072
  8.7 54.5 %shard_map.95 = (f32[2,16,1024]{2,1,0:T(8,128)S(1)}, f32[2,128,512]{2,1,0:T(8,128)S(1)}) custom-call(f32[2,128,512]{2,1,0:T(8,128)S(1)} %copy-done.1, f32[2,128,512]{2,1,0:T(8,128)S(1)} %copy-done.2, f32[6,1024]{1,0:T(8,128)S(1)} %copy-done.3, f32[8,1024]{1,0:T(8,128)S(1)} %copy-done.4, f32[316,16,128]{2,1,0:T(8,128)S(1)} %bitcast.5, ...), custom_call_target="tpu_custom_call" | custom-call | tf_op jit(solution)/shard_map/pallas_call | solution.py:467
  63.2 0.7 %copy.15 = f32[2,16,1024]{2,1,0:T(8,128)} copy(f32[2,16,1024]{2,1,0:T(8,128)S(1)} %get-tuple-element.4) | data formatting | bytes 262144
  63.9 0.8 %copy.16 = f32[2,128,512]{2,1,0:T(8,128)} copy(f32[2,128,512]{2,1,0:T(8,128)S(1)} %get-tuple-element.5) | data formatting | bytes 1048576
Async XLA Ops:
  2.7 1.7 %copy-start = (f32[316,2,1024]{2,1,0:T(2,128)S(1)}, f32[316,2,1024]{2,1,0:T(2,128)}, u32[]{:S(2)}) copy-start(f32[316,2,1024]{2,1,0:T(2,128)} %param.12) | copy-start | bytes 7766020
  4.4 1.0 %copy-start.1 = (f32[2,128,512]{2,1,0:T(8,128)S(1)}, f32[2,128,512]{2,1,0:T(8,128)}, u32[]{:S(2)}) copy-start(f32[2,128,512]{2,1,0:T(8,128)} %cp.1) | copy-start | bytes 1572868
  5.5 1.0 %copy-start.2 = (f32[2,128,512]{2,1,0:T(8,128)S(1)}, f32[2,128,512]{2,1,0:T(8,128)}, u32[]{:S(2)}) copy-start(f32[2,128,512]{2,1,0:T(8,128)} %cl.1) | copy-start | bytes 1572868
  6.5 0.8 %copy-start.3 = (f32[6,1024]{1,0:T(8,128)S(1)}, f32[6,1024]{1,0:T(8,128)}, u32[]{:S(2)}) copy-start(f32[6,1024]{1,0:T(8,128)} %w.1) | copy-start | bytes 73732
  7.3 0.8 %copy-start.4 = (f32[8,1024]{1,0:T(8,128)S(1)}, f32[8,1024]{1,0:T(8,128)}, u32[]{:S(2)}) copy-start(f32[8,1024]{1,0:T(8,128)} %ph.1) | copy-start | bytes 98308
  8.0 0.7 %copy-start.5 = (s32[512]{0:T(512)S(1)}, s32[512]{0:T(512)}, u32[]{:S(2)}) copy-start(s32[512]{0:T(512)} %length.1) | copy-start | bytes 6148

commit v2 on v1

--- a/solution.py
+++ b/solution.py
@@ -97,14 +97,15 @@
     z_low = (z + 31) % 32
     z_high = (z + 1) % 32
 
-    first_row = pl.multiple_of(me * PAR, PAR)
+    first_col = pl.multiple_of(128 * (me // 8), 128)
+    own_col = PAR * (me % 8)
     loads = [
         pltpu.make_async_copy(w, wv, load_sem.at[0]),
         pltpu.make_async_copy(ph, phv, load_sem.at[1]),
         pltpu.make_async_copy(cp, xpad.at[:, :, pl.ds(128, 512)], load_sem.at[2]),
-        pltpu.make_async_copy(oper.at[pl.ds(first_row, PAR)], opv, load_sem.at[3]),
+        pltpu.make_async_copy(oper.at[:, pl.ds(first_col, 128)], opv, load_sem.at[3]),
         pltpu.make_async_copy(length, lens, load_sem.at[4]),
-        pltpu.make_async_copy(part.at[pl.ds(first_row, PAR)], pidx, load_sem.at[5]),
+        pltpu.make_async_copy(part.at[:, pl.ds(first_col, 128)], pidx, load_sem.at[5]),
         pltpu.make_async_copy(t, tv, load_sem.at[6]),
         pltpu.make_async_copy(cl, clv, load_sem.at[7]),
     ]
@@ -196,7 +197,7 @@
                 agg[b, odd, 1, pl.ds(p, 1), :] = jnp.sum(imag, axis=0, keepdims=True)
             return 0
 
-        lax.fori_loop(0, PAR, one, 0)
+        lax.fori_loop(0, PAR, one, 0, unroll=4)
         chunk, place = CHUNK_OF[b]
         for c in range(2):
             for i in range(2):
@@ -300,10 +301,10 @@
             first = [jnp.zeros((8, 128), jnp.float32) for _ in range(2)]
             second = [jnp.zeros((8, 128), jnp.float32) for _ in range(2)]
             for slot in range(LMAX):
-                source = gathered[h][pidx[q, slot]]
-                o = oidx[q, slot]
-                first[slot % 2] += tables[h][o, 0:8, :] * source
-                second[slot % 2] += tables[h][o, 8:16, :] * source
+                source = gathered[h][pidx[slot, own_col + q]]
+                table = tables[h][oidx[slot, own_col + q]]
+                first[slot % 2] += table[0:8] * source
+                second[slot % 2] += table[8:16] * source
             cross = second[0] + second[1]
             swapped = jnp.where(subs() % 2 == 0, pltpu.roll(cross, 7, 0), pltpu.roll(cross, 1, 0))
             incoming[h][pl.ds(pl.multiple_of(8 * q, 8), 8), :] = first[0] + first[1] + swapped
@@ -333,14 +334,18 @@
     own(1)
     loads[3].wait()
     loads[4].wait()
-    live = jnp.zeros((PAR, LMAX), jnp.int32)
-    row = lax.broadcasted_iota(jnp.int32, (PAR, LMAX), 0)
+    loads[5].wait()
+    live = jnp.zeros((1, 128), jnp.int32)
+    column = lax.broadcasted_iota(jnp.int32, (1, 128), 1)
     for i in range(PAR):
-        live = jnp.where(row == i, lens[me * PAR + i], live)
-    slot = lax.broadcasted_iota(jnp.int32, (PAR, LMAX), 1)
+        live = jnp.where(column == own_col + i, lens[me * PAR + i], live)
+    slot = lax.broadcasted_iota(jnp.int32, (LMAX, 128), 0)
     opm[...] = jnp.where(slot < live, opv[...], NT)
-    to_smem = pltpu.make_async_copy(opm, oidx, index_sem)
-    to_smem.start()
+    to_smem = [
+        pltpu.make_async_copy(opm, oidx, index_sem.at[0]),
+    ]
+    for copy in to_smem:
+        copy.start()
 
     for halo in halos:
         halo.wait_recv()
@@ -388,8 +393,8 @@
     col_far(0, 2)
     col_near(1, 2)
     col_far(0, 3)
-    to_smem.wait()
-    loads[5].wait()
+    for copy in to_smem:
+        copy.wait()
     twin_all(0)
     translate(0, 0, 4)
     col_near(1, 3)
@@ -448,7 +453,7 @@
             out1[c, rows, :] = total
         return 0
 
-    lax.fori_loop(0, PAR, disaggregate, 0)
+    lax.fori_loop(0, PAR, disaggregate, 0, unroll=2)
 
     for halo in halos:
         halo.wait_send()
@@ -490,17 +495,17 @@
             pltpu.VMEM((2, 6, 8, 768), f32),
             pltpu.VMEM((4, 2, 2, 16, 128), f32),
             pltpu.VMEM((6, 2, 2, 16, 128), f32),
-            pltpu.VMEM((16, 64), jnp.int32),
-            pltpu.VMEM((16, 64), jnp.int32),
-            pltpu.SMEM((16, 64), jnp.int32),
-            pltpu.SMEM((16, 64), jnp.int32),
+            pltpu.VMEM((64, 128), jnp.int32),
+            pltpu.VMEM((64, 128), jnp.int32),
+            pltpu.SMEM((64, 128), jnp.int32),
+            pltpu.SMEM((64, 128), jnp.int32),
             pltpu.SMEM((512,), jnp.int32),
             pltpu.VMEM((2, 2, 8, 128), f32),
             pltpu.VMEM((2, 2, 8, 128), f32),
             pltpu.VMEM((2, 8, 128), f32),
             pltpu.VMEM((2, 8, 128), f32),
             pltpu.SemaphoreType.DMA((8,)),
-            pltpu.SemaphoreType.DMA,
+            pltpu.SemaphoreType.DMA((2,)),
             pltpu.SemaphoreType.DMA((2,)),
             pltpu.SemaphoreType.DMA((2, 3)),
             pltpu.SemaphoreType.DMA((2, 4, 3)),
@@ -511,9 +516,9 @@
             pltpu.SemaphoreType.DMA((2,)),
         ],
         compiler_params=pltpu.CompilerParams(
-            collective_id=0, has_side_effects=True, vmem_limit_bytes=48 * 1024 * 1024
+            collective_id=0, has_side_effects=True, vmem_limit_bytes=56 * 1024 * 1024
         ),
-    )(child_pattern, child_local, interp_weight, child_phase, folded, partners, operator_id, list_len)
+    )(child_pattern, child_local, interp_weight, child_phase, folded, partners.T, operator_id.T, list_len)
 
 
 def solution(mesh):

time: 65.1 us -> 56.4 us (0.87)
  local copies, waits for them, and re-layouts: 9.51 us -> 3.44 us
  Pallas kernels: 54.5 us -> 52.1 us
    unnamed x16 -> x2, local copies, waits for them, and re-layouts: 9.51 us -> 3.44 us
    pallas_call x1, Pallas kernels: 54.5 us -> 52.1 us  [local(): pl.pallas_call(kernel, out_shape=(jax.ShapeDtypeStruct((2, PAR, 1024), f3...]
where the time goes in v2:
time: 56.4 us; the launch traced here: 56.2 us
  Pallas kernels  52.1 us (92%)
  local copies, waits for them, and re-layouts  3.44 us (6%)
  between operations  0.64 us (1%)
    pallas_call x1, Pallas kernels, local(): pl.pallas_call(kernel, out_shape=(jax.ShapeDtypeStruct((2, PAR, 1024), f3...  52.1 us
    unnamed x2, local copies, waits for them, and re-layouts  3.44 us

profile of v2, /device:TPU:1, one launch (start us, length us, event | category | flops | bytes accessed | tf_op | source)
XLA Modules:
  0.0 56.2 jit_solution(16693491092120372303)
XLA Ops:
  0.6 52.1 %shard_map.95 = (f32[2,16,1024]{2,1,0:T(8,128)}, f32[2,128,512]{2,1,0:T(8,128)}) custom-call(f32[2,128,512]{2,1,0:T(8,128)} %cp.1, f32[2,128,512]{2,1,0:T(8,128)} %cl.1, f32[6,1024]{1,0:T(8,128)} %w.1, f32[8,1024]{1,0:T(8,128)} %ph.1, f32[316,16,128]{2,1,0:T(8,128)} %bitcast.7, s32[64,512]{1,0:T(8,128)} %bitcast.8, s32[64,512]{1,0:T(8,128)} %bitcast.9, ...), custom_call_target="tpu_custom_call" | custom-call | tf_op jit(solution)/shard_map/pallas_call | solution.py:472
  52.8 1.6 %copy.13 = f32[2,16,1024]{2,1,0:T(8,128)} copy(f32[2,16,1024]{2,1,0:T(8,128)} %get-tuple-element.4) | data formatting | bytes 262144
  54.4 1.9 %copy.14 = f32[2,128,512]{2,1,0:T(8,128)} copy(f32[2,128,512]{2,1,0:T(8,128)} %get-tuple-element.5) | data formatting | bytes 1048576

commit v3 on v2

--- a/solution.py
+++ b/solution.py
@@ -463,13 +463,31 @@
     sent_all(1)
 
 
+def hand_over(parents, children, out0, out1, held0, held1, sem):
+    pieces = []
+    for c in range(2):
+        pieces.append((parents.at[c], held0.at[c], out0.at[c]))
+        for i in range(4):
+            rows = pl.ds(32 * i, 32)
+            pieces.append((children.at[c, rows], held1.at[c, rows], out1.at[c, rows]))
+    reads = [pltpu.make_async_copy(a, b, sem.at[0, k]) for k, (a, b, _) in enumerate(pieces)]
+    writes = [pltpu.make_async_copy(b, c, sem.at[1, k]) for k, (_, b, c) in enumerate(pieces)]
+    for read in reads:
+        read.start()
+    for read, write in zip(reads, writes):
+        read.wait()
+        write.start()
+    for write in writes:
+        write.wait()
+
+
 def local(child_pattern, child_local, interp_weight, child_phase, translator, partners, operator_id, list_len):
     operators = translator.shape[0]
     folded = translator.reshape(operators, 2, 8, 128).transpose(0, 2, 1, 3).reshape(operators, 16, 128)
     f32 = jnp.float32
     any_spec = pl.BlockSpec(memory_space=pl.ANY)
     vmem_spec = pl.BlockSpec(memory_space=pltpu.VMEM)
-    return pl.pallas_call(
+    parents, children = pl.pallas_call(
         kernel,
         out_shape=(
             jax.ShapeDtypeStruct((2, PAR, 1024), f32),
@@ -519,6 +537,21 @@
             collective_id=0, has_side_effects=True, vmem_limit_bytes=56 * 1024 * 1024
         ),
     )(child_pattern, child_local, interp_weight, child_phase, folded, partners.T, operator_id.T, list_len)
+    return pl.pallas_call(
+        hand_over,
+        out_shape=(
+            jax.ShapeDtypeStruct((2, PAR, 1024), f32),
+            jax.ShapeDtypeStruct((2, 128, 512), f32),
+        ),
+        in_specs=[any_spec] * 2,
+        out_specs=(any_spec, any_spec),
+        scratch_shapes=[
+            pltpu.VMEM((2, PAR, 1024), f32),
+            pltpu.VMEM((2, 128, 512), f32),
+            pltpu.SemaphoreType.DMA((2, 10)),
+        ],
+        compiler_params=pltpu.CompilerParams(vmem_limit_bytes=56 * 1024 * 1024),
+    )(parents, children)
 
 
 def solution(mesh):

time: 56.4 us -> 54.9 us (0.973)
  local copies, waits for them, and re-layouts: 3.44 us -> 0 us
  Pallas kernels: 52.1 us -> 54.1 us
    unnamed x2 -> x0, local copies, waits for them, and re-layouts: 3.44 us -> none
    pallas_call x0 -> x1, Pallas kernels: none -> 1.92 us  [local(): pl.pallas_call(hand_over, out_shape=(jax.ShapeDtypeStruct((2, PAR, 1024),...]
where the time goes in v3:
time: 54.9 us; the launch traced here: 54.7 us
  Pallas kernels  54.1 us (99%)
  between operations  0.64 us (1%)
    pallas_call x1, Pallas kernels, local(): pl.pallas_call(kernel, out_shape=(jax.ShapeDtypeStruct((2, PAR, 1024), f3...  52.1 us
    pallas_call x1, Pallas kernels, local(): pl.pallas_call(hand_over, out_shape=(jax.ShapeDtypeStruct((2, PAR, 1024),...  1.92 us

profile of v3, /device:TPU:1, one launch (start us, length us, event | category | flops | bytes accessed | tf_op | source)
XLA Modules:
  0.0 54.7 jit_solution(9621515187275650257)
XLA Ops:
  0.6 52.1 %shard_map.95 = (f32[2,16,1024]{2,1,0:T(8,128)}, f32[2,128,512]{2,1,0:T(8,128)}) custom-call(f32[2,128,512]{2,1,0:T(8,128)} %cp.1, f32[2,128,512]{2,1,0:T(8,128)} %cl.1, f32[6,1024]{1,0:T(8,128)} %w.1, f32[8,1024]{1,0:T(8,128)} %ph.1, f32[316,16,128]{2,1,0:T(8,128)} %bitcast.7, s32[64,512]{1,0:T(8,128)} %bitcast.8, s32[64,512]{1,0:T(8,128)} %bitcast.9, ...), custom_call_target="tpu_custom_call" | custom-call | tf_op jit(solution)/shard_map/pallas_call | solution.py:490
  52.8 1.9 %shard_map.96 = (f32[2,16,1024]{2,1,0:T(8,128)}, f32[2,128,512]{2,1,0:T(8,128)}) custom-call(f32[2,16,1024]{2,1,0:T(8,128)} %get-tuple-element.4.parents, f32[2,128,512]{2,1,0:T(8,128)} %get-tuple-element.5.children), custom_call_target="tpu_custom_call" | custom-call | tf_op jit(solution)/shard_map/pallas_call | solution.py:540

commit v4 on v3

--- a/solution.py
+++ b/solution.py
@@ -197,7 +197,7 @@
                 agg[b, odd, 1, pl.ds(p, 1), :] = jnp.sum(imag, axis=0, keepdims=True)
             return 0
 
-        lax.fori_loop(0, PAR, one, 0, unroll=4)
+        lax.fori_loop(0, PAR, one, 0, unroll=True)
         chunk, place = CHUNK_OF[b]
         for c in range(2):
             for i in range(2):

time: 54.9 us -> 54.2 us (0.987)
  Pallas kernels: 54.1 us -> 53.4 us
    pallas_call x1, Pallas kernels: 52.1 us -> 51.4 us  [local(): pl.pallas_call(kernel, out_shape=(jax.ShapeDtypeStruct((2, PAR, 1024), f3...]
where the time goes in v4:
time: 54.2 us; the launch traced here: 54 us
  Pallas kernels  53.4 us (99%)
  between operations  0.64 us (1%)
    pallas_call x1, Pallas kernels, local(): pl.pallas_call(kernel, out_shape=(jax.ShapeDtypeStruct((2, PAR, 1024), f3...  51.4 us
    pallas_call x1, Pallas kernels, local(): pl.pallas_call(hand_over, out_shape=(jax.ShapeDtypeStruct((2, PAR, 1024),...  1.92 us

profile of v4, /device:TPU:1, one launch (start us, length us, event | category | flops | bytes accessed | tf_op | source)
XLA Modules:
  0.0 54.0 jit_solution(1017213735321032642)
XLA Ops:
  0.6 51.4 %shard_map.95 = (f32[2,16,1024]{2,1,0:T(8,128)}, f32[2,128,512]{2,1,0:T(8,128)}) custom-call(f32[2,128,512]{2,1,0:T(8,128)} %cp.1, f32[2,128,512]{2,1,0:T(8,128)} %cl.1, f32[6,1024]{1,0:T(8,128)} %w.1, f32[8,1024]{1,0:T(8,128)} %ph.1, f32[316,16,128]{2,1,0:T(8,128)} %bitcast.7, s32[64,512]{1,0:T(8,128)} %bitcast.8, s32[64,512]{1,0:T(8,128)} %bitcast.9, ...), custom_call_target="tpu_custom_call" | custom-call | tf_op jit(solution)/shard_map/pallas_call | solution.py:490
  52.1 1.9 %shard_map.96 = (f32[2,16,1024]{2,1,0:T(8,128)}, f32[2,128,512]{2,1,0:T(8,128)}) custom-call(f32[2,16,1024]{2,1,0:T(8,128)} %get-tuple-element.4.parents, f32[2,128,512]{2,1,0:T(8,128)} %get-tuple-element.5.children), custom_call_target="tpu_custom_call" | custom-call | tf_op jit(solution)/shard_map/pallas_call | solution.py:540
